TPU v7x, 32 devices: a whole 2x2x4 slice. The times are simulated.
32 devices in a mesh: tok: 4 (over z), row: 4 (over y, core), col: 2 (over x).
Axes of the slice: x: 2, y: 2, z: 4, core: 2. Of those that a mesh axis runs over, the one named last changes fastest.
Arguments:
- activations: bfloat16 [1024, 8192], P('tok', 'row'), may hold values from -8 to 8
- gradients: bfloat16 [1024, 8192], P('tok', 'col'), may hold values from -8 to 8
- act_basis: bfloat16 [8192, 8192], P('row', ('tok', 'col')), may hold values from -1 to 1
- grad_basis: bfloat16 [8192, 8192], P('col', 'row'), may hold values from -1 to 1
- eigen_noise: float32 [8192, 8192], P('row', ('tok', 'col')), may hold values from -6 to 6
Outputs:
- scales: float32 [8192, 8192], P('row', ('tok', 'col'))
- output_shift: bfloat16 [1024, 8192], P('tok', 'col')
All inputs are finite; a program needn't handle non-finite values.
Results may differ from a plain program's by a relative error of at most 0.0064.
Values may be sent and summed in bfloat16 or wider, within the bound.
A program may use at most 128 MiB of HBM per device.

v0:
```python
import jax
import jax.numpy as jnp
from jax import lax
from jax.sharding import PartitionSpec as P

damping = 0.1


def contract(former, latter, former_dim, latter_dim):
    return lax.dot_general(
        former,
        latter,
        (((former_dim,), (latter_dim,)), ((), ())),
        preferred_element_type=jnp.float32,
    )


def shards(activations, gradients, act_basis, grad_basis, eigen_noise):
    half = jnp.bfloat16
    token_count = activations.shape[0] * lax.axis_size("tok")
    acts = lax.all_gather(activations, "tok", axis=0, tiled=True)
    grad_part = contract(gradients, grad_basis, 1, 0).astype(half)
    grad_proj = lax.psum(grad_part, "col").astype(jnp.float32)
    grad_sq = (grad_proj * grad_proj).astype(half)
    grad_all = lax.all_gather(grad_sq, "tok", axis=0, tiled=True)
    act_wide = lax.psum(contract(acts, act_basis, 1, 0), "row")
    act_half = act_wide.astype(half)
    act_sq = (act_wide * act_wide).astype(half)
    scales = contract(grad_all, act_sq, 0, 0) / token_count
    scaled = (eigen_noise * lax.rsqrt(token_count * (scales + damping))).astype(half)
    hidden_part = contract(act_half, scaled, 1, 1).astype(half)
    hidden_part = lax.psum_scatter(hidden_part, "tok", scatter_dimension=0, tiled=True)
    hidden = lax.psum(hidden_part, "col")
    output_part = contract(hidden, grad_basis, 1, 1).astype(half)
    output_shift = lax.psum(output_part, "row")
    return (scales, output_shift)


def solution(mesh):
    in_specs = (
        P("tok", "row"),
        P("tok", "col"),
        P("row", ("tok", "col")),
        P("col", "row"),
        P("row", ("tok", "col")),
    )
    out_specs = (P("row", ("tok", "col")), P("tok", "col"))
    return jax.shard_map(shards, mesh=mesh, in_specs=in_specs, out_specs=out_specs, check_vma=False)
```

profile of v0, /device:TPU:0, one launch (start us, length us, event | category | flops | bytes accessed | tf_op | source)
XLA Modules:
  0.0 487.4 jit_solution(1072756323985646304)
XLA Ops:
  8.0 0.0 copy-start
  8.0 0.0 all-reduce.5.cloned.1.call-start
  8.1 1.5 copy-done
  9.6 9.2 %convolution_convert_fusion.1 = bf16[256,2048]{1,0:T(8,128)(2,1)} fusion(bf16[256,4096]{1,0:T(8,128)(2,1)S(1)} %copy-done, bf16[4096,2048]{1,0:T(8,128)(2,1)} %param.8), kind=kOutput, calls=%fused_computation.8 | convolution fusion | flops 4295491584 | bytes 19922944 | tf_op jit(solution)/shard_map/dot_general | solution.py:10
  18.8 0.0 all-reduce.5.cloned.1.call-update
  18.8 0.0 all-gather.5.cloned.1.call-start
  18.9 0.5 all-gather.5.cloned.1.call-update
  19.4 0.0 all-gather.3.cloned.1.call-start
  19.5 42.3 %all-reduce.5.cloned.1.call-done = bf16[256,2048]{1,0:T(8,128)(2,1)} async-done(((bf16[256,2048]{1,0:T(8,128)(2,1)}), bf16[256,2048]{1,0:T(8,128)(2,1)}) %all-reduce.5.cloned.1.call-update) | async-done | bytes 1048592 | tf_op jit(solution)/shard_map/psum | solution.py:23
  61.8 2.4 multiply_convert_fusion.6
  64.2 0.0 all-gather.3.cloned.1.call-update
  64.2 0.0 all-reduce.7.cloned.1.call-start
  64.3 39.9 %all-gather.5.cloned.1.call-done = bf16[1024,2048]{1,0:T(8,128)(2,1)} async-done(((bf16[256,2048]{1,0:T(8,128)(2,1)}), bf16[1024,2048]{1,0:T(8,128)(2,1)}) %all-gather.5.cloned.1.call-update) | async-done | bytes 4194320 | tf_op jit(solution)/shard_map/all_gather | solution.py:21
  104.2 10.0 %fusion.7 = f32[1024,1024]{1,0:T(8,128)} fusion(bf16[1024,2048]{1,0:T(8,128)(2,1)} %all-gather.5.cloned.1.call-done, bf16[2048,1024]{1,0:T(8,128)(2,1)} %param.7), kind=kOutput, calls=%fused_computation.13 | convolution fusion | flops 4294967296 | bytes 12582912 | tf_op jit(solution)/shard_map/dot_general | solution.py:10
  114.2 0.0 all-reduce.7.cloned.1.call-update
  114.2 0.2 reduce-scatter.2.cloned.1.call-start
  114.4 71.0 %all-gather.3.cloned.1.call-done = bf16[1024,2048]{1,0:T(8,128)(2,1)} async-done(((bf16[256,2048]{1,0:T(8,128)(2,1)}), bf16[1024,2048]{1,0:T(8,128)(2,1)}) %all-gather.3.cloned.1.call-update) | async-done | bytes 4194320 | tf_op jit(solution)/shard_map/all_gather | solution.py:25
  185.4 86.8 %all-reduce.7.cloned.1.call-done = f32[1024,1024]{1,0:T(8,128)} async-done(((f32[1024,1024]{1,0:T(8,128)}), f32[1024,1024]{1,0:T(8,128)}) %all-reduce.7.cloned.1.call-update) | async-done | bytes 4194320 | tf_op jit(solution)/shard_map/psum | solution.py:26
  272.2 0.0 copy-start.2
  272.2 11.6 %convolution_multiply_fusion = f32[2048,1024]{1,0:T(8,128)} fusion(bf16[1024,2048]{1,0:T(8,128)(2,1)} %all-gather.3.cloned.1.call-done, f32[1024,1024]{1,0:T(8,128)} %all-reduce.7.cloned.1.call-done), kind=kOutput, calls=%fused_computation.2 | convolution fusion | flops 4299161600 | bytes 16777216 | tf_op jit(solution)/shard_map/dot_general | solution.py:10
  283.8 0.0 copy-done.2
  283.8 11.9 %fusion.3 = bf16[1024,2048]{1,0:T(8,128)(2,1)} fusion(f32[2048,1024]{1,0:T(8,128)} %param.9, f32[2048,1024]{1,0:T(8,128)} %convolution_multiply_fusion, f32[1024,1024]{1,0:T(8,128)S(1)} %copy-done.2), kind=kOutput, calls=%fused_computation.7 | convolution fusion | flops 4306501632 | bytes 25165824 | tf_op jit(solution)/shard_map/dot_general | solution.py:10
  295.7 0.0 reduce-scatter.2.cloned.1.call-update
  295.7 0.0 all-reduce.9.cloned.1.call-start
  295.7 77.0 %reduce-scatter.2.cloned.1.call-done = bf16[256,2048]{1,0:T(8,128)(2,1)} async-done(((bf16[1024,2048]{1,0:T(8,128)(2,1)}), bf16[256,2048]{1,0:T(8,128)(2,1)}) %reduce-scatter.2.cloned.1.call-update) | async-done | bytes 1048592 | tf_op jit(solution)/shard_map/reduce_scatter | solution.py:32
  372.7 0.0 all-reduce.9.cloned.1.call-update
  372.7 0.0 all-reduce.11.cloned.1.call-start
  372.8 40.5 %all-reduce.9.cloned.1.call-done = bf16[256,2048]{1,0:T(8,128)(2,1)} async-done(((bf16[256,2048]{1,0:T(8,128)(2,1)}), bf16[256,2048]{1,0:T(8,128)(2,1)}) %all-reduce.9.cloned.1.call-update) | async-done | bytes 1048592 | tf_op jit(solution)/shard_map/psum | solution.py:33
  413.3 0.0 copy-start.1
  413.3 12.1 %convolution_convert_fusion = bf16[256,4096]{1,0:T(8,128)(2,1)} fusion(bf16[256,2048]{1,0:T(8,128)(2,1)} %all-reduce.9.cloned.1.call-done, bf16[4096,2048]{1,0:T(8,128)(2,1)} %param.8), kind=kOutput, calls=%fused_computation.1 | convolution fusion | flops 4296015872 | bytes 19922944 | tf_op jit(solution)/shard_map/dot_general | solution.py:10
  425.4 0.0 all-reduce.11.cloned.1.call-update
  425.4 51.3 %all-reduce.11.cloned.1.call-done = bf16[256,4096]{1,0:T(8,128)(2,1)} async-done(((bf16[256,4096]{1,0:T(8,128)(2,1)}), bf16[256,4096]{1,0:T(8,128)(2,1)}) %all-reduce.11.cloned.1.call-update) | async-done | bytes 2097168 | tf_op jit(solution)/shard_map/psum | solution.py:35
  476.7 3.1 copy.11
  479.9 0.0 copy-done.1
Async XLA Ops:
  8.0 1.6 copy-start
  8.0 53.8 %all-reduce.5.cloned.1.call-start = ((), (), s32[]{:S(2)}) async-start(), calls=%async_computation.1 | async-start | bytes 2097152 | tf_op jit(solution)/shard_map/psum | solution.py:23
  18.8 85.4 %all-gather.5.cloned.1.call-start = ((), (), s32[]{:S(2)}) async-start(), calls=%async_computation.3 | async-start | bytes 5242880 | tf_op jit(solution)/shard_map/all_gather | solution.py:21
  19.4 166.0 %all-gather.3.cloned.1.call-start = ((), (), s32[]{:S(2)}) async-start(), calls=%async_computation.2 | async-start | bytes 5242880 | tf_op jit(solution)/shard_map/all_gather | solution.py:25
  64.2 208.0 %all-reduce.7.cloned.1.call-start = ((), (), s32[]{:S(2)}) async-start(), calls=%async_computation.4 | async-start | bytes 8388608 | tf_op jit(solution)/shard_map/psum | solution.py:26
  114.2 258.5 %reduce-scatter.2.cloned.1.call-start = ((), (), s32[]{:S(2)}) async-start(), calls=%async_computation.5 | async-start | bytes 5242880 | tf_op jit(solution)/shard_map/reduce_scatter | solution.py:32
  272.2 11.6 %copy-start.2 = (f32[1024,1024]{1,0:T(8,128)S(1)}, f32[1024,1024]{1,0:T(8,128)}, u32[]{:S(2)}) copy-start(f32[1024,1024]{1,0:T(8,128)} %all-reduce.7.cloned.1.call-done) | copy-start | bytes 12582916
  295.7 117.6 %all-reduce.9.cloned.1.call-start = ((), (), s32[]{:S(2)}) async-start(), calls=%async_computation.6 | async-start | bytes 2097152 | tf_op jit(solution)/shard_map/psum | solution.py:33
  372.7 104.0 %all-reduce.11.cloned.1.call-start = ((), (), s32[]{:S(2)}) async-start(), calls=%async_computation.7 | async-start | bytes 4194304 | tf_op jit(solution)/shard_map/psum | solution.py:35
  413.3 66.5 %copy-start.1 = (bf16[256,4096]{1,0:T(8,128)(2,1)S(1)}, bf16[256,4096]{1,0:T(8,128)(2,1)}, u32[]{:S(2)}) copy-start(bf16[256,4096]{1,0:T(8,128)(2,1)} %param.6) | copy-start | bytes 6291460
Sparse Core Ops, SparseCore 0:
  18.9 42.7 all-reduce.4
  372.9 40.4 all-reduce.8
Sparse Core Ops, SparseCore 1:
  20.9 83.3 all-gather.4
  106.3 79.1 all-gather.2
  188.4 83.8 all-reduce.6
  295.8 76.9 reduce-scatter.1
  425.5 51.1 all-reduce.10
where the time goes:
time: 488 us; the launch traced here: 487 us
  waiting for transfers between devices  409 us (84%)
  matrix products  54.7 us (11%)
  between operations  15.7 us (3%)
    psum x1, waiting for transfers between devices, shards(): act_wide = lax.psum(contract(acts, act_basis, 1, 0), 'row')  86.8 us
    reduce_scatter x1, waiting for transfers between devices, shards(): lax.psum_scatter(hidden_part, 'tok', scatter_dimension=0, tiled=True)  77 us
    all_gather x1, waiting for transfers between devices, shards(): grad_all = lax.all_gather(grad_sq, 'tok', axis=0, tiled=True)  71 us
    dot_general x5, matrix products, contract(): lax.dot_general(former, latter, (((former_dim,), (latter_dim,)), ((), ())...  54.7 us
    psum x1, waiting for transfers between devices, shards(): output_shift = lax.psum(output_part, 'row')  51.3 us
    psum x1, waiting for transfers between devices, shards(): grad_proj = lax.psum(grad_part, 'col').astype(jnp.float32)  42.3 us
    psum x1, waiting for transfers between devices, shards(): hidden = lax.psum(hidden_part, 'col')  40.5 us
    all_gather x1, waiting for transfers between devices, shards(): acts = lax.all_gather(activations, 'tok', axis=0, tiled=True)  39.9 us
  transfers between devices with their start and end apart: 7, of which 7 were waited for; matrix products, arithmetic and copies ran while one was open for 3% of the time, Pallas kernels for 0%

commit v1 on v0

v1 whole, which is shorter than its diff:
```python
import functools

import jax
import jax.numpy as jnp
from jax import lax
from jax.experimental import pallas as pl
from jax.experimental.pallas import tpu as pltpu
from jax.sharding import PartitionSpec as P

damping = 0.1
half = jnp.bfloat16
wide = jnp.float32
MESH = pl.DeviceIdType.MESH
VMEM_BYTES = 60 * 1024 * 1024


def contract(former, latter, former_dim, latter_dim):
    return lax.dot_general(
        former,
        latter,
        (((former_dim,), (latter_dim,)), ((), ())),
        preferred_element_type=jnp.float32,
    )


def remote(src, dst, send_sem, recv_sem, where):
    return pltpu.make_async_remote_copy(
        src_ref=src, dst_ref=dst, send_sem=send_sem, recv_sem=recv_sem,
        device_id=where, device_id_type=MESH,
    )


def arrived(ref, sem, where):
    remote(ref, ref, sem, sem, where).wait_recv()


def enter(nt, nr, nc):
    t, r, c = (lax.axis_index(a) for a in ("tok", "row", "col"))
    barrier = pltpu.get_barrier_semaphore()
    places = [{"tok": lax.rem(t + nt - 1, nt)}]
    places += [{"col": lax.rem(c + k, nc)} for k in range(1, nc)]
    places += [{"row": lax.rem(r + k, nr)} for k in range(1, nr)]
    for place in places:
        pl.semaphore_signal(barrier, inc=1, device_id=place, device_id_type=MESH)
    pl.semaphore_wait(barrier, len(places))
    return t, r, c


def project_kernel(nt, nr, nc, act_hbm, grad_hbm, ab_hbm, gb_hbm, act_half, grad_all,
                   acts, grads, ab, gb, gpart, gown, grecv, part, precv,
                   l_sem, g_send, g_recv, a_send, a_recv, ax_send, ax_recv,
                   c_send, c_recv, cx_send, cx_recv, rs_send, rs_recv, ag_send, ag_recv):
    R = grads.shape[0]
    Fp, Q = ab.shape[1:]
    Pp = gb.shape[2]
    S = R // nr
    t0, c0 = lax.axis_index("tok"), lax.axis_index("col")
    locals_ = []

    def local(src, dst):
        copy = pltpu.make_async_copy(src, dst, l_sem.at[len(locals_)])
        copy.start()
        locals_.append(copy)
        return copy

    act_in = [local(act_hbm.at[:, pl.ds(k * Fp, Fp)], acts.at[k, t0]) for k in range(nc)]
    grad_in = local(grad_hbm, grads)
    gb_in = []
    for k in range(nc):
        peer = lax.rem(c0 + k + 1, nc)
        gb_in.append(local(gb_hbm.at[:, pl.ds(pl.multiple_of(peer * Pp, 128), Pp)], gb.at[k]))
    ab_in = [local(ab_hbm.at[pl.ds(k * Fp, Fp), :], ab.at[k]) for k in range(nc)]

    t, r, c = enter(nt, nr, nc)
    right = {"tok": lax.rem(t + 1, nt)}
    cols = [lax.rem(c + k, nc) for k in range(1, nc)]
    rows = [lax.rem(r + k, nr) for k in range(1, nr)]
    sent = []

    def send(*args):
        copy = remote(*args)
        copy.start()
        sent.append(copy)

    def tok_block(s):
        return lax.rem(t - s + nt, nt)

    def ring(buf, s, send_sem, recv_sem):
        piece = buf.at[c, tok_block(s)]
        send(piece, piece, send_sem.at[s], recv_sem.at[s], right)

    def spread(buf, s, slot, send_sem, recv_sem):
        piece = buf.at[c, tok_block(s)]
        for k, peer in enumerate(cols):
            send(piece, piece, send_sem.at[slot, k], recv_sem.at[slot, c], {"col": peer})

    def ring_recv(buf, s, send_sem, recv_sem, x_send, x_recv):
        arrived(buf.at[c, tok_block(s + 1)], recv_sem.at[s], right)
        if s < nt - 2:
            ring(buf, s + 1, send_sem, recv_sem)
        spread(buf, s + 1, s, x_send, x_recv)

    for copy in act_in:
        copy.wait()
    ring(acts, 0, a_send, a_recv)

    W = min(256, Pp)
    grad_in.wait()
    for k, peer in enumerate(cols):
        gb_in[k].wait()

        @pl.loop(0, Pp // W)
        def _(j, k=k, peer=peer):
            at = pl.ds(pl.multiple_of(j * W, W), W)
            gpart[peer, :, at] = contract(grads[...], gb[k, :, at], 1, 0).astype(half)

        send(gpart.at[peer], grecv.at[c], g_send.at[k], g_recv.at[c], {"col": peer})
    ring_recv(acts, 0, a_send, a_recv, ax_send, ax_recv)
    gb_in[nc - 1].wait()

    @pl.loop(0, Pp // W)
    def _(j):
        at = pl.ds(pl.multiple_of(j * W, W), W)
        gown[:, at] = contract(grads[...], gb[nc - 1, :, at], 1, 0)

    V = min(256, Q)

    def act_block(u):
        b = tok_block(u)
        if u > 0:
            for peer in cols:
                arrived(acts.at[peer, b], ax_recv.at[u - 1, peer], {"col": peer})

        @pl.loop(0, Q // V)
        def _(j):
            at = pl.ds(pl.multiple_of(j * V, V), V)
            total = contract(acts[0, b], ab[0, :, at], 1, 0)
            for k in range(1, nc):
                total = total + contract(acts[k, b], ab[k, :, at], 1, 0)
            part[b, :, at] = total.astype(half)

        for k, peer in enumerate(rows):
            send(part.at[b, pl.ds(pl.multiple_of(peer * S, 16), S)], precv.at[u, r],
                 rs_send.at[u, k], rs_recv.at[u, r], {"row": peer})

    def reduce_block(u):
        b = tok_block(u)
        at = pl.ds(pl.multiple_of(r * S, 16), S)
        total = part[b, at, :].astype(wide)
        for peer in rows:
            arrived(precv.at[u, peer], rs_recv.at[u, peer], {"row": peer})
            total = total + precv[u, peer].astype(wide)
        act_half[b, at, :] = total.astype(half)
        for k, peer in enumerate(rows):
            piece = act_half.at[b, at]
            send(piece, piece, ag_send.at[u, k], ag_recv.at[u, r], {"row": peer})

    for copy in ab_in:
        copy.wait()
    act_block(0)
    for peer in cols:
        arrived(grecv.at[peer], g_recv.at[peer], {"col": peer})

    @pl.loop(0, Pp // W)
    def _(j):
        at = pl.ds(pl.multiple_of(j * W, W), W)
        total = gown[:, at]
        for peer in cols:
            total = total + grecv[peer, :, at].astype(wide)
        grad_all[c, t, :, at] = (total * total).astype(half)

    ring(grad_all, 0, c_send, c_recv)
    spread(grad_all, 0, nt - 1, cx_send, cx_recv)
    for s in range(1, nt - 1):
        ring_recv(acts, s, a_send, a_recv, ax_send, ax_recv)
        act_block(s)
        ring_recv(grad_all, s - 1, c_send, c_recv, cx_send, cx_recv)
        reduce_block(s - 1)
    act_block(nt - 1)
    ring_recv(grad_all, nt - 2, c_send, c_recv, cx_send, cx_recv)
    reduce_block(nt - 2)
    reduce_block(nt - 1)
    for u in range(nt):
        for peer in rows:
            piece = act_half.at[tok_block(u), pl.ds(pl.multiple_of(peer * S, 16), S)]
            arrived(piece, ag_recv.at[u, peer], {"row": peer})
        for peer in cols:
            slot = (u + nt - 1) % nt
            arrived(grad_all.at[peer, tok_block(u)], cx_recv.at[slot, peer], {"col": peer})
    for copy in sent:
        copy.wait_send()


def output_kernel(nt, nr, nc, hp, gb_hbm, out, xr, zs, zr, hid, gb, osend, orecv,
                  l_sem, x_send, x_recv, z_send, z_recv, h_send, h_recv,
                  rs_send, rs_recv, ag_send, ag_recv):
    R, Pp = hid.shape[1:]
    chunks, _, Oc = osend.shape
    S = R // nr
    gb_in = pltpu.make_async_copy(gb_hbm, gb, l_sem)
    gb_in.start()
    t, r, c = enter(nt, nr, nc)
    right = {"tok": lax.rem(t + 1, nt)}
    cols = [lax.rem(c + k, nc) for k in range(1, nc)]
    rows = [lax.rem(r + k, nr) for k in range(1, nr)]
    sent = []

    def send(*args):
        copy = remote(*args)
        copy.start()
        sent.append(copy)

    def tok_block(u):
        return lax.rem(t - 1 - u + 2 * nt, nt)

    def piece_of(peer):
        return pl.ds(pl.multiple_of(peer * Pp, 128), Pp)

    for u in range(nt):
        for k, peer in enumerate(cols):
            send(hp.at[tok_block(u), :, piece_of(peer)], xr.at[u, c],
                 x_send.at[u, k], x_recv.at[u, c], {"col": peer})
    for u in range(nt):
        b = tok_block(u)
        for peer in cols:
            arrived(xr.at[u, peer], x_recv.at[u, peer], {"col": peer})
        if u > 0:
            arrived(zr.at[u - 1], z_recv.at[u - 1], right)

        @pl.loop(0, R // 32)
        def _(i):
            at = pl.ds(pl.multiple_of(i * 32, 32), 32)
            total = hp[b, at, piece_of(c)].astype(wide)
            for peer in cols:
                total = total + xr[u, peer, at, :].astype(wide)
            if u > 0:
                total = total + zr[u - 1, at, :].astype(wide)
            if u < nt - 1:
                zs[u, at, :] = total.astype(half)
            else:
                hid[c, at, :] = total.astype(half)

        if u < nt - 1:
            send(zs.at[u], zr.at[u], z_send.at[u], z_recv.at[u], right)
    for k, peer in enumerate(cols):
        send(hid.at[c], hid.at[c], h_send.at[k], h_recv.at[c], {"col": peer})
    gb_in.wait()
    for peer in cols:
        arrived(hid.at[peer], h_recv.at[peer], {"col": peer})
    W = min(256, Oc)

    def columns(j):
        return pl.ds(j * Oc, Oc)

    def reduce_chunk(j):
        at = pl.ds(pl.multiple_of(r * S, 16), S)
        total = osend[j, at, :].astype(wide)
        for peer in rows:
            arrived(orecv.at[j, peer], rs_recv.at[j, peer], {"row": peer})
            total = total + orecv[j, peer].astype(wide)
        out[at, columns(j)] = total.astype(half)
        for k, peer in enumerate(rows):
            piece = out.at[at, columns(j)]
            send(piece, piece, ag_send.at[j, k], ag_recv.at[j, r], {"row": peer})

    for j in range(chunks):
        @pl.loop(0, Oc // W)
        def _(i):
            at = pl.ds(pl.multiple_of(j * Oc + i * W, W), W)
            total = contract(hid[0], gb[at, pl.ds(0, Pp)], 1, 1)
            for k in range(1, nc):
                total = total + contract(hid[k], gb[at, pl.ds(k * Pp, Pp)], 1, 1)
            osend[j, :, pl.ds(pl.multiple_of(i * W, W), W)] = total.astype(half)

        for k, peer in enumerate(rows):
            send(osend.at[j, pl.ds(pl.multiple_of(peer * S, 16), S)], orecv.at[j, r],
                 rs_send.at[j, k], rs_recv.at[j, r], {"row": peer})
        if j > 1:
            reduce_chunk(j - 2)
    reduce_chunk(chunks - 2)
    reduce_chunk(chunks - 1)
    for j in range(chunks):
        for peer in rows:
            piece = out.at[pl.ds(pl.multiple_of(peer * S, 16), S), columns(j)]
            arrived(piece, ag_recv.at[j, peer], {"row": peer})
    for copy in sent:
        copy.wait_send()


def project(nt, nr, nc, activations, gradients, act_basis, grad_basis):
    R, F = activations.shape
    Q = act_basis.shape[1]
    G, Pn = grad_basis.shape
    Fp, Pp, S = F // nc, Pn // nc, R // nr
    dma = pltpu.SemaphoreType.DMA
    return pl.pallas_call(
        functools.partial(project_kernel, nt, nr, nc),
        out_shape=(
            jax.ShapeDtypeStruct((nt, R, Q), half),
            jax.ShapeDtypeStruct((nc, nt, R, Pp), half),
        ),
        in_specs=[pl.BlockSpec(memory_space=pl.ANY)] * 4,
        out_specs=[pl.BlockSpec(memory_space=pltpu.VMEM)] * 2,
        scratch_shapes=[
            pltpu.VMEM((nc, nt, R, Fp), half),
            pltpu.VMEM((R, G), half),
            pltpu.VMEM((nc, Fp, Q), half),
            pltpu.VMEM((nc, G, Pp), half),
            pltpu.VMEM((nc, R, Pp), half),
            pltpu.VMEM((R, Pp), wide),
            pltpu.VMEM((nc, R, Pp), half),
            pltpu.VMEM((nt, R, Q), half),
            pltpu.VMEM((nt, nr, S, Q), half),
            dma((3 * nc + 1,)),
            dma((nc,)), dma((nc,)),
            dma((nt,)), dma((nt,)), dma((nt, nc)), dma((nt, nc)),
            dma((nt,)), dma((nt,)), dma((nt, nc)), dma((nt, nc)),
            dma((nt, nr)), dma((nt, nr)), dma((nt, nr)), dma((nt, nr)),
        ],
        compiler_params=pltpu.CompilerParams(
            collective_id=0, has_side_effects=True, vmem_limit_bytes=VMEM_BYTES
        ),
        cost_estimate=pl.CostEstimate(
            flops=2 * R * G * Pn + 2 * nt * R * F * Q, bytes_accessed=2 * (G * Pn + F * Q), transcendentals=0
        ),
    )(activations, gradients, act_basis, grad_basis)


def shift(nt, nr, nc, hidden_part, grad_basis):
    R = hidden_part.shape[1]
    G, Pn = grad_basis.shape
    Pp, S = Pn // nc, R // nr
    chunks = 4
    Oc = G // chunks
    dma = pltpu.SemaphoreType.DMA
    return pl.pallas_call(
        functools.partial(output_kernel, nt, nr, nc),
        out_shape=jax.ShapeDtypeStruct((R, G), half),
        in_specs=[pl.BlockSpec(memory_space=pltpu.VMEM), pl.BlockSpec(memory_space=pl.ANY)],
        out_specs=pl.BlockSpec(memory_space=pltpu.VMEM),
        scratch_shapes=[
            pltpu.VMEM((nt, nc, R, Pp), half),
            pltpu.VMEM((nt, R, Pp), half),
            pltpu.VMEM((nt, R, Pp), half),
            pltpu.VMEM((nc, R, Pp), half),
            pltpu.VMEM((G, Pn), half),
            pltpu.VMEM((chunks, R, Oc), half),
            pltpu.VMEM((chunks, nr, S, Oc), half),
            dma,
            dma((nt, nc)), dma((nt, nc)), dma((nt,)), dma((nt,)), dma((nc,)), dma((nc,)),
            dma((chunks, nr)), dma((chunks, nr)), dma((chunks, nr)), dma((chunks, nr)),
        ],
        compiler_params=pltpu.CompilerParams(
            collective_id=1, has_side_effects=True, vmem_limit_bytes=VMEM_BYTES
        ),
        cost_estimate=pl.CostEstimate(flops=2 * R * G * Pn, bytes_accessed=2 * G * Pn, transcendentals=0),
    )(hidden_part, grad_basis)


def shards(nt, nr, nc, activations, gradients, act_basis, grad_basis, eigen_noise):
    R = activations.shape[0]
    token_count = R * nt
    act_half, grad_all = project(nt, nr, nc, activations, gradients, act_basis, grad_basis)
    act_half = act_half.reshape(token_count, -1)
    act_wide = act_half.astype(wide)
    act_sq = (act_wide * act_wide).astype(half)
    grad_all = grad_all.reshape(nc, token_count, -1)
    scales = lax.dot_general(
        grad_all, act_sq, (((1,), (0,)), ((), ())), preferred_element_type=wide
    ).reshape(eigen_noise.shape) / token_count
    scaled = (eigen_noise * lax.rsqrt(token_count * (scales + damping))).astype(half)
    hidden_part = contract(act_half, scaled, 1, 1).astype(half).reshape(nt, R, -1)
    return (scales, shift(nt, nr, nc, hidden_part, grad_basis))


def solution(mesh):
    in_specs = (
        P("tok", "row"),
        P("tok", "col"),
        P("row", ("tok", "col")),
        P("col", "row"),
        P("row", ("tok", "col")),
    )
    out_specs = (P("row", ("tok", "col")), P("tok", "col"))
    sizes = (mesh.shape["tok"], mesh.shape["row"], mesh.shape["col"])
    return jax.shard_map(
        functools.partial(shards, *sizes), mesh=mesh, in_specs=in_specs, out_specs=out_specs, check_vma=False
    )
```

time: 488 us -> 248 us (0.51)
  waiting for transfers between devices: 409 us -> 0 us
  Pallas kernels: 0 us -> 218 us
  matrix products: 54.7 us -> 16.7 us
  between operations: 15.7 us -> 0.67 us
  local copies, waits for them, and re-layouts: 4.68 us -> 11.2 us
    psum x4 -> x0, waiting for transfers between devices: 221 us -> none  [the longest x1 86.8 us: shards(): act_wide = lax.psum(contract(acts, act_basis, 1, 0), 'row')]
    pallas_call x0 -> x2, Pallas kernels: none -> 218 us  [the longest x1 113 us: shift(): pl.pallas_call(functools.partial(output_kernel, nt, nr, nc), out_shape=ja...]
    all_gather x2 -> x0, waiting for transfers between devices: 111 us -> none  [the longest x1 71 us: shards(): grad_all = lax.all_gather(grad_sq, 'tok', axis=0, tiled=True)]
    reduce_scatter x1 -> x0, waiting for transfers between devices: 77 us -> none  [shards(): lax.psum_scatter(hidden_part, 'tok', scatter_dimension=0, tiled=True)]
    dot_general x5 -> x1, matrix products: 54.7 us -> 10 us  [contract(): lax.dot_general(former, latter, (((former_dim,), (latter_dim,)), ((), ())...]
    dot_general x0 -> x1, matrix products: none -> 6.74 us  [shards(): lax.dot_general(grad_all, act_sq, (((1,), (0,)), ((), ())), preferred_ele...]
    reshape x0 -> x1, local copies, waits for them, and re-layouts: none -> 6.34 us  [shards(): grad_all = grad_all.reshape(nc, token_count, -1)]
  transfers between devices with their start and end apart: 7 -> 0, of which waited for: 7 -> 0; matrix products, arithmetic and copies ran while one was open for 3% -> 0% of each run, Pallas kernels for 0% -> 0%
where the time goes in v1:
time: 248 us; the launch traced here: 247 us
  Pallas kernels  218 us (88%)
  matrix products  16.7 us (7%)
  local copies, waits for them, and re-layouts  11.2 us (5%)
    pallas_call x1, Pallas kernels, shift(): pl.pallas_call(functools.partial(output_kernel, nt, nr, nc), out_shape=ja...  113 us
    pallas_call x1, Pallas kernels, project(): pl.pallas_call(functools.partial(project_kernel, nt, nr, nc), out_shape=(...  105 us
    dot_general x1, matrix products, contract(): lax.dot_general(former, latter, (((former_dim,), (latter_dim,)), ((), ())...  10 us
    dot_general x1, matrix products, shards(): lax.dot_general(grad_all, act_sq, (((1,), (0,)), ((), ())), preferred_ele...  6.74 us
    reshape x1, local copies, waits for them, and re-layouts, shards(): grad_all = grad_all.reshape(nc, token_count, -1)  6.34 us

profile of v1, /device:TPU:0, one launch (start us, length us, event | category | flops | bytes accessed | tf_op | source)
XLA Modules:
  0.0 247.1 jit_solution(10307681875707593695)
XLA Ops:
  0.6 104.7 %shard_map.68 = (bf16[4,256,1024]{2,1,0:T(8,128)(2,1)}, bf16[2,4,256,1024]{3,2,1,0:T(8,128)(2,1)}) custom-call(bf16[256,2048]{1,0:T(8,128)(2,1)} %act_hbm.1, bf16[256,4096]{1,0:T(8,128)(2,1)} %grad_hbm.1, bf16[2048,1024]{1,0:T(8,128)(2,1)} %ab_hbm.1, bf16[4096,2048]{1,0:T(8,128)(2,1)} %gb_hbm.3), custom_call_target="tpu_custom_call" | custom-call | flops 8589934592 | bytes 20971520 | tf_op jit(solution)/shard_map/pallas_call | solution.py:296
  105.3 0.0 copy-start.1
  105.3 6.3 %copy.7 = bf16[2,1024,1024]{1,2,0:T(8,128)(2,1)} copy(bf16[2,1024,1024]{2,1,0:T(8,128)(2,1)} %bitcast.10) | data formatting | bytes 8388608 | tf_op jit(solution)/shard_map/reshape | solution.py:367
  111.6 0.0 copy-start
  111.6 0.0 copy-done.1
  111.6 0.0 slice-start
  111.7 0.5 multiply_convert_fusion.2
  112.2 1.7 copy-done
  113.8 0.0 slice-start.1
  113.8 6.7 %convolution_multiply_fusion = f32[2048,1024]{1,0:T(8,128)} fusion(bf16[2048,1024]{1,0:T(8,128)(2,1)S(1)} %bitcast.11, bf16[1024,1024]{1,0:T(8,128)(2,1)S(1)} %bitcast.14), kind=kOutput, calls=%fused_computation.1 | convolution fusion | flops 4297064448 | bytes 14680064 | tf_op jit(solution)/shard_map/dot_general | solution.py:368
  120.6 0.0 slice-done
  120.6 0.0 slice-done.1
  120.6 10.0 %fusion.3 = bf16[1024,2048]{1,0:T(8,128)(2,1)} fusion(bf16[1024,1024]{1,0:T(8,128)(2,1)S(1)} %bitcast.13, f32[2048,1024]{1,0:T(8,128)S(1)} %bitcast.16, f32[2048,1024]{1,0:T(8,128)} %convolution_multiply_fusion), kind=kOutput, calls=%fused_computation.6 | convolution fusion | flops 4305453056 | bytes 23068672 | tf_op jit(solution)/shard_map/dot_general | solution.py:18
  130.6 113.4 %shard_map.69 = bf16[256,4096]{1,0:T(8,128)(2,1)} custom-call(bf16[4,256,2048]{2,1,0:T(8,128)(2,1)} %bitcast.12, bf16[4096,2048]{1,0:T(8,128)(2,1)} %gb_hbm.3), custom_call_target="tpu_custom_call" | custom-call | flops 4294967296 | bytes 16777216 | tf_op jit(solution)/shard_map/pallas_call | solution.py:336
  244.0 3.1 %copy.9 = bf16[256,4096]{1,0:T(8,128)(2,1)} copy(bf16[256,4096]{1,0:T(8,128)(2,1)} %shard_map.69) | data formatting | bytes 4194304
  (1 shorter events, 0.0 us)
Async XLA Ops:
  105.3 6.4 %copy-start.1 = (bf16[4,256,1024]{2,1,0:T(8,128)(2,1)S(1)}, bf16[4,256,1024]{2,1,0:T(8,128)(2,1)}, u32[]{:S(2)}) copy-start(bf16[4,256,1024]{2,1,0:T(8,128)(2,1)} %get-tuple-element.5) | copy-start | bytes 6291460
  111.6 2.2 copy-start
  111.6 8.9 %slice-start = ((s8[8388608]{0:T(1024)(128)(4,1)}), s8[4194304]{0:T(1024)(128)(4,1)S(1)}, s32[]{:S(2)}) async-start(s8[8388608]{0:T(1024)(128)(4,1)} %bitcast.15), calls=%async_computation | async-start | bytes 8388608
  113.8 6.8 %slice-start.1 = ((s8[8388608]{0:T(1024)(128)(4,1)}), s8[4194304]{0:T(1024)(128)(4,1)S(1)}, s32[]{:S(2)}) async-start(s8[8388608]{0:T(1024)(128)(4,1)} %bitcast.15), calls=%async_computation.1 | async-start | bytes 8388608

commit v2 on v1

--- a/solution.py
+++ b/solution.py
@@ -48,7 +48,7 @@
 
 def project_kernel(nt, nr, nc, act_hbm, grad_hbm, ab_hbm, gb_hbm, act_half, grad_all,
                    acts, grads, ab, gb, gpart, gown, grecv, part, precv,
-                   l_sem, g_send, g_recv, a_send, a_recv, ax_send, ax_recv,
+                   l_sem, g_send, g_recv, a_send, a_recv, az_send, az_recv, ax_send, ax_recv,
                    c_send, c_recv, cx_send, cx_recv, rs_send, rs_recv, ag_send, ag_recv):
     R = grads.shape[0]
     Fp, Q = ab.shape[1:]
@@ -94,11 +94,12 @@
         for k, peer in enumerate(cols):
             send(piece, piece, send_sem.at[slot, k], recv_sem.at[slot, c], {"col": peer})
 
-    def ring_recv(buf, s, send_sem, recv_sem, x_send, x_recv):
+    def ring_recv(buf, s, send_sem, recv_sem, x_send, x_recv, skip=False):
         arrived(buf.at[c, tok_block(s + 1)], recv_sem.at[s], right)
         if s < nt - 2:
             ring(buf, s + 1, send_sem, recv_sem)
-        spread(buf, s + 1, s, x_send, x_recv)
+        if not skip:
+            spread(buf, s + 1, s, x_send, x_recv)
 
     for copy in act_in:
         copy.wait()
@@ -115,7 +116,9 @@
             gpart[peer, :, at] = contract(grads[...], gb[k, :, at], 1, 0).astype(half)
 
         send(gpart.at[peer], grecv.at[c], g_send.at[k], g_recv.at[c], {"col": peer})
-    ring_recv(acts, 0, a_send, a_recv, ax_send, ax_recv)
+    for peer in cols:
+        send(acts.at[peer, t], acts.at[peer, t], az_send.at[peer], az_recv.at[peer], right)
+    ring_recv(acts, 0, a_send, a_recv, ax_send, ax_recv, True)
     gb_in[nc - 1].wait()
 
     @pl.loop(0, Pp // W)
@@ -127,7 +130,10 @@
 
     def act_block(u):
         b = tok_block(u)
-        if u > 0:
+        if u == 1:
+            for peer in cols:
+                arrived(acts.at[peer, b], az_recv.at[peer], right)
+        if u > 1:
             for peer in cols:
                 arrived(acts.at[peer, b], ax_recv.at[u - 1, peer], {"col": peer})
 
@@ -191,9 +197,9 @@
         copy.wait_send()
 
 
-def output_kernel(nt, nr, nc, hp, gb_hbm, out, xr, zs, zr, hid, gb, osend, orecv,
+def output_kernel(nt, nr, nc, act_half, scaled, gb_hbm, out, hp, xr, zs, zr, hid, gb, osend, orecv,
                   l_sem, x_send, x_recv, z_send, z_recv, h_send, h_recv,
-                  rs_send, rs_recv, ag_send, ag_recv):
+                  rs_send, rs_recv, ag_send, ag_recv, fw_send):
     R, Pp = hid.shape[1:]
     chunks, _, Oc = osend.shape
     S = R // nr
@@ -213,13 +219,20 @@
     def tok_block(u):
         return lax.rem(t - 1 - u + 2 * nt, nt)
 
-    def piece_of(peer):
-        return pl.ds(pl.multiple_of(peer * Pp, 128), Pp)
+    W = min(256, Pp)
+
+    def hidden_tile(b, piece, j):
+        at = pl.ds(pl.multiple_of(piece * Pp + j * W, W), W)
+        return contract(act_half[b], scaled[at, :], 1, 1)
 
     for u in range(nt):
         for k, peer in enumerate(cols):
-            send(hp.at[tok_block(u), :, piece_of(peer)], xr.at[u, c],
-                 x_send.at[u, k], x_recv.at[u, c], {"col": peer})
+            @pl.loop(0, Pp // W)
+            def _(j, u=u, k=k, peer=peer):
+                at = pl.ds(pl.multiple_of(j * W, W), W)
+                hp[u, k, :, at] = hidden_tile(tok_block(u), peer, j).astype(half)
+
+            send(hp.at[u, k], xr.at[u, c], x_send.at[u, k], x_recv.at[u, c], {"col": peer})
     for u in range(nt):
         b = tok_block(u)
         for peer in cols:
@@ -227,18 +240,18 @@
         if u > 0:
             arrived(zr.at[u - 1], z_recv.at[u - 1], right)
 
-        @pl.loop(0, R // 32)
-        def _(i):
-            at = pl.ds(pl.multiple_of(i * 32, 32), 32)
-            total = hp[b, at, piece_of(c)].astype(wide)
+        @pl.loop(0, Pp // W)
+        def _(j, u=u, b=b):
+            at = pl.ds(pl.multiple_of(j * W, W), W)
+            total = hidden_tile(b, c, j)
             for peer in cols:
-                total = total + xr[u, peer, at, :].astype(wide)
+                total = total + xr[u, peer, :, at].astype(wide)
             if u > 0:
-                total = total + zr[u - 1, at, :].astype(wide)
+                total = total + zr[u - 1, :, at].astype(wide)
             if u < nt - 1:
-                zs[u, at, :] = total.astype(half)
+                zs[u, :, at] = total.astype(half)
             else:
-                hid[c, at, :] = total.astype(half)
+                hid[c, :, at] = total.astype(half)
 
         if u < nt - 1:
             send(zs.at[u], zr.at[u], z_send.at[u], z_recv.at[u], right)
@@ -247,7 +260,9 @@
     gb_in.wait()
     for peer in cols:
         arrived(hid.at[peer], h_recv.at[peer], {"col": peer})
-    W = min(256, Oc)
+    V = min(256, Oc)
+    twin = r + 1 - 2 * lax.rem(r, 2)
+    far = [lax.rem(r + 2 * k, nr) for k in range(1, nr // 2)]
 
     def columns(j):
         return pl.ds(j * Oc, Oc)
@@ -259,18 +274,24 @@
             arrived(orecv.at[j, peer], rs_recv.at[j, peer], {"row": peer})
             total = total + orecv[j, peer].astype(wide)
         out[at, columns(j)] = total.astype(half)
-        for k, peer in enumerate(rows):
+        for k, peer in enumerate(far + [twin]):
             piece = out.at[at, columns(j)]
             send(piece, piece, ag_send.at[j, k], ag_recv.at[j, r], {"row": peer})
 
+    def forward_chunk(j):
+        for k, peer in enumerate(far):
+            piece = out.at[pl.ds(pl.multiple_of(peer * S, 16), S), columns(j)]
+            arrived(piece, ag_recv.at[j, peer], {"row": peer})
+            send(piece, piece, fw_send.at[j, k], ag_recv.at[j, peer], {"row": twin})
+
     for j in range(chunks):
-        @pl.loop(0, Oc // W)
-        def _(i):
-            at = pl.ds(pl.multiple_of(j * Oc + i * W, W), W)
+        @pl.loop(0, Oc // V)
+        def _(i, j=j):
+            at = pl.ds(pl.multiple_of(j * Oc + i * V, V), V)
             total = contract(hid[0], gb[at, pl.ds(0, Pp)], 1, 1)
             for k in range(1, nc):
                 total = total + contract(hid[k], gb[at, pl.ds(k * Pp, Pp)], 1, 1)
-            osend[j, :, pl.ds(pl.multiple_of(i * W, W), W)] = total.astype(half)
+            osend[j, :, pl.ds(pl.multiple_of(i * V, V), V)] = total.astype(half)
 
         for k, peer in enumerate(rows):
             send(osend.at[j, pl.ds(pl.multiple_of(peer * S, 16), S)], orecv.at[j, r],
@@ -278,9 +299,13 @@
         if j > 1:
             reduce_chunk(j - 2)
     reduce_chunk(chunks - 2)
+    for j in range(chunks - 2):
+        forward_chunk(j)
     reduce_chunk(chunks - 1)
+    forward_chunk(chunks - 2)
+    forward_chunk(chunks - 1)
     for j in range(chunks):
-        for peer in rows:
+        for peer in [twin] + [lax.rem(twin + 2 * k, nr) for k in range(1, nr // 2)]:
             piece = out.at[pl.ds(pl.multiple_of(peer * S, 16), S), columns(j)]
             arrived(piece, ag_recv.at[j, peer], {"row": peer})
     for copy in sent:
@@ -313,7 +338,7 @@
             pltpu.VMEM((nt, nr, S, Q), half),
             dma((3 * nc + 1,)),
             dma((nc,)), dma((nc,)),
-            dma((nt,)), dma((nt,)), dma((nt, nc)), dma((nt, nc)),
+            dma((nt,)), dma((nt,)), dma((nc,)), dma((nc,)), dma((nt, nc)), dma((nt, nc)),
             dma((nt,)), dma((nt,)), dma((nt, nc)), dma((nt, nc)),
             dma((nt, nr)), dma((nt, nr)), dma((nt, nr)), dma((nt, nr)),
         ],
@@ -326,8 +351,43 @@
     )(activations, gradients, act_basis, grad_basis)
 
 
-def shift(nt, nr, nc, hidden_part, grad_basis):
-    R = hidden_part.shape[1]
+def scale_kernel(token_count, grad, act_half, noise, scales, scaled, act_sq):
+    @pl.when((pl.program_id(0) == 0) & (pl.program_id(1) == 0))
+    def _():
+        value = act_half[...].astype(wide)
+        act_sq[...] = (value * value).astype(half)
+
+    total = contract(grad[0], act_sq[...], 0, 0) / token_count
+    scales[...] = total
+    scaled[...] = (noise[...] * lax.rsqrt(token_count * (total + damping))).astype(half)
+
+
+def scale(act_half, grad_all, noise):
+    Pn, Q = noise.shape
+    nc, tokens, Pp = grad_all.shape
+    W = min(256, Pp)
+    steps = Pp // W
+    strip = pl.BlockSpec((W, Q), lambda c, j: (c * steps + j, 0))
+    return pl.pallas_call(
+        functools.partial(scale_kernel, tokens),
+        grid=(nc, steps),
+        out_shape=(jax.ShapeDtypeStruct((Pn, Q), wide), jax.ShapeDtypeStruct((Pn, Q), half)),
+        in_specs=[
+            pl.BlockSpec((1, tokens, W), lambda c, j: (c, 0, j)),
+            pl.BlockSpec((tokens, Q), lambda c, j: (0, 0)),
+            strip,
+        ],
+        out_specs=[strip, strip],
+        scratch_shapes=[pltpu.VMEM((tokens, Q), half)],
+        compiler_params=pltpu.CompilerParams(vmem_limit_bytes=VMEM_BYTES),
+        cost_estimate=pl.CostEstimate(
+            flops=2 * tokens * Pn * Q, bytes_accessed=10 * Pn * Q, transcendentals=Pn * Q
+        ),
+    )(grad_all, act_half, noise)
+
+
+def shift(nt, nr, nc, act_half, scaled, grad_basis):
+    R = act_half.shape[1]
     G, Pn = grad_basis.shape
     Pp, S = Pn // nc, R // nr
     chunks = 4
@@ -336,9 +396,10 @@
     return pl.pallas_call(
         functools.partial(output_kernel, nt, nr, nc),
         out_shape=jax.ShapeDtypeStruct((R, G), half),
-        in_specs=[pl.BlockSpec(memory_space=pltpu.VMEM), pl.BlockSpec(memory_space=pl.ANY)],
+        in_specs=[pl.BlockSpec(memory_space=pltpu.VMEM)] * 2 + [pl.BlockSpec(memory_space=pl.ANY)],
         out_specs=pl.BlockSpec(memory_space=pltpu.VMEM),
         scratch_shapes=[
+            pltpu.VMEM((nt, nc - 1, R, Pp), half),
             pltpu.VMEM((nt, nc, R, Pp), half),
             pltpu.VMEM((nt, R, Pp), half),
             pltpu.VMEM((nt, R, Pp), half),
@@ -348,29 +409,21 @@
             pltpu.VMEM((chunks, nr, S, Oc), half),
             dma,
             dma((nt, nc)), dma((nt, nc)), dma((nt,)), dma((nt,)), dma((nc,)), dma((nc,)),
-            dma((chunks, nr)), dma((chunks, nr)), dma((chunks, nr)), dma((chunks, nr)),
+            dma((chunks, nr)), dma((chunks, nr)), dma((chunks, nr)), dma((chunks, nr)), dma((chunks, nr)),
         ],
         compiler_params=pltpu.CompilerParams(
             collective_id=1, has_side_effects=True, vmem_limit_bytes=VMEM_BYTES
         ),
         cost_estimate=pl.CostEstimate(flops=2 * R * G * Pn, bytes_accessed=2 * G * Pn, transcendentals=0),
-    )(hidden_part, grad_basis)
+    )(act_half, scaled, grad_basis)
 
 
 def shards(nt, nr, nc, activations, gradients, act_basis, grad_basis, eigen_noise):
-    R = activations.shape[0]
-    token_count = R * nt
+    token_count = activations.shape[0] * nt
     act_half, grad_all = project(nt, nr, nc, activations, gradients, act_basis, grad_basis)
-    act_half = act_half.reshape(token_count, -1)
-    act_wide = act_half.astype(wide)
-    act_sq = (act_wide * act_wide).astype(half)
     grad_all = grad_all.reshape(nc, token_count, -1)
-    scales = lax.dot_general(
-        grad_all, act_sq, (((1,), (0,)), ((), ())), preferred_element_type=wide
-    ).reshape(eigen_noise.shape) / token_count
-    scaled = (eigen_noise * lax.rsqrt(token_count * (scales + damping))).astype(half)
-    hidden_part = contract(act_half, scaled, 1, 1).astype(half).reshape(nt, R, -1)
-    return (scales, shift(nt, nr, nc, hidden_part, grad_basis))
+    scales, scaled = scale(act_half.reshape(token_count, -1), grad_all, eigen_noise)
+    return (scales, shift(nt, nr, nc, act_half, scaled, grad_basis))
 
 
 def solution(mesh):

time: 248 us -> 235 us (0.948); the launches traced: 247 us -> 231 us
  matrix products: 16.7 us -> 0 us
  Pallas kernels: 218 us -> 227 us
  local copies, waits for them, and re-layouts: 11.2 us -> 3.13 us
    dot_general x2 -> x0, matrix products: 16.7 us -> none  [the longest x1 10 us: contract(): lax.dot_general(former, latter, (((former_dim,), (latter_dim,)), ((), ())...]
    pallas_call x0 -> x1, Pallas kernels: none -> 15.1 us  [scale(): pl.pallas_call(functools.partial(scale_kernel, tokens), grid=(nc, steps),...]
    reshape x1 -> x0, local copies, waits for them, and re-layouts: 6.34 us -> none  [shards(): grad_all = grad_all.reshape(nc, token_count, -1)]
    pallas_call x1, Pallas kernels: 113 us -> 109 us  [shift(): pl.pallas_call(functools.partial(output_kernel, nt, nr, nc), out_shape=ja...]
where the time goes in v2:
time: 235 us; the launch traced here: 231 us
  Pallas kernels  227 us (97%)
  local copies, waits for them, and re-layouts  3.13 us (1%)
    pallas_call x1, Pallas kernels, shift(): pl.pallas_call(functools.partial(output_kernel, nt, nr, nc), out_shape=ja...  109 us
    pallas_call x1, Pallas kernels, project(): pl.pallas_call(functools.partial(project_kernel, nt, nr, nc), out_shape=(...  104 us
    pallas_call x1, Pallas kernels, scale(): pl.pallas_call(functools.partial(scale_kernel, tokens), grid=(nc, steps),...  15.1 us

profile of v2, /device:TPU:0, one launch (start us, length us, event | category | flops | bytes accessed | tf_op | source)
XLA Modules:
  0.0 231.0 jit_solution(5159315443655137682)
XLA Ops:
  0.6 103.6 %shard_map.68 = (bf16[4,256,1024]{2,1,0:T(8,128)(2,1)}, bf16[2,4,256,1024]{3,2,1,0:T(8,128)(2,1)}) custom-call(bf16[256,2048]{1,0:T(8,128)(2,1)} %act_hbm.1, bf16[256,4096]{1,0:T(8,128)(2,1)} %grad_hbm.1, bf16[2048,1024]{1,0:T(8,128)(2,1)} %ab_hbm.1, bf16[4096,2048]{1,0:T(8,128)(2,1)} %gb_hbm.3), custom_call_target="tpu_custom_call" | custom-call | flops 8589934592 | bytes 20971520 | tf_op jit(solution)/shard_map/pallas_call | solution.py:321
  104.3 15.1 %shard_map.69 = (f32[2048,1024]{1,0:T(8,128)}, bf16[2048,1024]{1,0:T(8,128)(2,1)}) custom-call(bf16[2,1024,1024]{2,1,0:T(8,128)(2,1)} %bitcast.3, bf16[1024,1024]{1,0:T(8,128)(2,1)} %bitcast.2, f32[2048,1024]{1,0:T(8,128)} %noise.1), custom_call_target="tpu_custom_call" | custom-call | flops 4294967296 | bytes 20971520 | tf_op jit(solution)/shard_map/pallas_call | solution.py:371
  119.3 108.6 %shard_map.70 = bf16[256,4096]{1,0:T(8,128)(2,1)} custom-call(bf16[4,256,1024]{2,1,0:T(8,128)(2,1)} %get-tuple-element.7.act_half, bf16[2048,1024]{1,0:T(8,128)(2,1)} %get-tuple-element.9.scaled, bf16[4096,2048]{1,0:T(8,128)(2,1)} %gb_hbm.3), custom_call_target="tpu_custom_call" | custom-call | flops 4294967296 | bytes 16777216 | tf_op jit(solution)/shard_map/pallas_call | solution.py:396
  227.9 3.1 %copy.8 = bf16[256,4096]{1,0:T(8,128)(2,1)} copy(bf16[256,4096]{1,0:T(8,128)(2,1)} %shard_map.70) | data formatting | bytes 4194304

commit v3 on v2

--- a/solution.py
+++ b/solution.py
@@ -54,6 +54,8 @@
     Fp, Q = ab.shape[1:]
     Pp = gb.shape[2]
     S = R // nr
+    Wp = gown.shape[2]
+    H = Pp // Wp
     t0, c0 = lax.axis_index("tok"), lax.axis_index("col")
     locals_ = []
 
@@ -85,46 +87,54 @@
     def tok_block(s):
         return lax.rem(t - s + nt, nt)
 
-    def ring(buf, s, send_sem, recv_sem):
-        piece = buf.at[c, tok_block(s)]
-        send(piece, piece, send_sem.at[s], recv_sem.at[s], right)
-
-    def spread(buf, s, slot, send_sem, recv_sem):
-        piece = buf.at[c, tok_block(s)]
+    def ring(buf, s, send_sem, recv_sem, h=0, H=1):
+        piece = buf.at[c * H + h, tok_block(s)]
+        send(piece, piece, send_sem.at[s * H + h], recv_sem.at[s * H + h], right)
+
+    def spread(buf, s, slot, send_sem, recv_sem, h=0, H=1):
+        piece = buf.at[c * H + h, tok_block(s)]
         for k, peer in enumerate(cols):
-            send(piece, piece, send_sem.at[slot, k], recv_sem.at[slot, c], {"col": peer})
-
-    def ring_recv(buf, s, send_sem, recv_sem, x_send, x_recv, skip=False):
-        arrived(buf.at[c, tok_block(s + 1)], recv_sem.at[s], right)
+            send(piece, piece, send_sem.at[slot * H + h, k], recv_sem.at[slot * H + h, c], {"col": peer})
+
+    def ring_recv(buf, s, send_sem, recv_sem, x_send, x_recv, skip=False, h=0, H=1):
+        arrived(buf.at[c * H + h, tok_block(s + 1)], recv_sem.at[s * H + h], right)
         if s < nt - 2:
-            ring(buf, s + 1, send_sem, recv_sem)
+            ring(buf, s + 1, send_sem, recv_sem, h, H)
         if not skip:
-            spread(buf, s + 1, s, x_send, x_recv)
+            spread(buf, s + 1, s, x_send, x_recv, h, H)
+
+    def squares_recv(s):
+        for h in range(H):
+            ring_recv(grad_all, s, c_send, c_recv, cx_send, cx_recv, h=h, H=H)
 
     for copy in act_in:
         copy.wait()
     ring(acts, 0, a_send, a_recv)
 
-    W = min(256, Pp)
+    W = min(256, Wp)
     grad_in.wait()
     for k, peer in enumerate(cols):
         gb_in[k].wait()
-
-        @pl.loop(0, Pp // W)
-        def _(j, k=k, peer=peer):
-            at = pl.ds(pl.multiple_of(j * W, W), W)
-            gpart[peer, :, at] = contract(grads[...], gb[k, :, at], 1, 0).astype(half)
-
-        send(gpart.at[peer], grecv.at[c], g_send.at[k], g_recv.at[c], {"col": peer})
+        for h in range(H):
+            @pl.loop(0, Wp // W)
+            def _(j, k=k, peer=peer, h=h):
+                at = pl.ds(pl.multiple_of(j * W, W), W)
+                tile = gb[k, :, pl.ds(pl.multiple_of(h * Wp + j * W, W), W)]
+                gpart[peer * H + h, :, at] = contract(grads[...], tile, 1, 0).astype(half)
+
+            send(gpart.at[peer * H + h], grecv.at[c * H + h],
+                 g_send.at[k * H + h], g_recv.at[c * H + h], {"col": peer})
     for peer in cols:
         send(acts.at[peer, t], acts.at[peer, t], az_send.at[peer], az_recv.at[peer], right)
     ring_recv(acts, 0, a_send, a_recv, ax_send, ax_recv, True)
     gb_in[nc - 1].wait()
 
-    @pl.loop(0, Pp // W)
-    def _(j):
-        at = pl.ds(pl.multiple_of(j * W, W), W)
-        gown[:, at] = contract(grads[...], gb[nc - 1, :, at], 1, 0)
+    for h in range(H):
+        @pl.loop(0, Wp // W)
+        def _(j, h=h):
+            at = pl.ds(pl.multiple_of(j * W, W), W)
+            tile = gb[nc - 1, :, pl.ds(pl.multiple_of(h * Wp + j * W, W), W)]
+            gown[h, :, at] = contract(grads[...], tile, 1, 0)
 
     V = min(256, Q)
 
@@ -163,27 +173,28 @@
 
     for copy in ab_in:
         copy.wait()
+    for h in range(H):
+        for peer in cols:
+            arrived(grecv.at[peer * H + h], g_recv.at[peer * H + h], {"col": peer})
+
+        @pl.loop(0, Wp // W)
+        def _(j, h=h):
+            at = pl.ds(pl.multiple_of(j * W, W), W)
+            total = gown[h, :, at]
+            for peer in cols:
+                total = total + grecv[peer * H + h, :, at].astype(wide)
+            grad_all[c * H + h, t, :, at] = (total * total).astype(half)
+
+        ring(grad_all, 0, c_send, c_recv, h, H)
+        spread(grad_all, 0, nt - 1, cx_send, cx_recv, h, H)
     act_block(0)
-    for peer in cols:
-        arrived(grecv.at[peer], g_recv.at[peer], {"col": peer})
-
-    @pl.loop(0, Pp // W)
-    def _(j):
-        at = pl.ds(pl.multiple_of(j * W, W), W)
-        total = gown[:, at]
-        for peer in cols:
-            total = total + grecv[peer, :, at].astype(wide)
-        grad_all[c, t, :, at] = (total * total).astype(half)
-
-    ring(grad_all, 0, c_send, c_recv)
-    spread(grad_all, 0, nt - 1, cx_send, cx_recv)
     for s in range(1, nt - 1):
         ring_recv(acts, s, a_send, a_recv, ax_send, ax_recv)
         act_block(s)
-        ring_recv(grad_all, s - 1, c_send, c_recv, cx_send, cx_recv)
+        squares_recv(s - 1)
         reduce_block(s - 1)
     act_block(nt - 1)
-    ring_recv(grad_all, nt - 2, c_send, c_recv, cx_send, cx_recv)
+    squares_recv(nt - 2)
     reduce_block(nt - 2)
     reduce_block(nt - 1)
     for u in range(nt):
@@ -192,7 +203,9 @@
             arrived(piece, ag_recv.at[u, peer], {"row": peer})
         for peer in cols:
             slot = (u + nt - 1) % nt
-            arrived(grad_all.at[peer, tok_block(u)], cx_recv.at[slot, peer], {"col": peer})
+            for h in range(H):
+                piece = grad_all.at[peer * H + h, tok_block(u)]
+                arrived(piece, cx_recv.at[slot * H + h, peer], {"col": peer})
     for copy in sent:
         copy.wait_send()
 
@@ -200,7 +213,9 @@
 def output_kernel(nt, nr, nc, act_half, scaled, gb_hbm, out, hp, xr, zs, zr, hid, gb, osend, orecv,
                   l_sem, x_send, x_recv, z_send, z_recv, h_send, h_recv,
                   rs_send, rs_recv, ag_send, ag_recv, fw_send):
-    R, Pp = hid.shape[1:]
+    R, Wp = hid.shape[1:]
+    H = hid.shape[0] // nc
+    Pp = H * Wp
     chunks, _, Oc = osend.shape
     S = R // nr
     gb_in = pltpu.make_async_copy(gb_hbm, gb, l_sem)
@@ -219,47 +234,50 @@
     def tok_block(u):
         return lax.rem(t - 1 - u + 2 * nt, nt)
 
-    W = min(256, Pp)
-
-    def hidden_tile(b, piece, j):
-        at = pl.ds(pl.multiple_of(piece * Pp + j * W, W), W)
+    W = min(256, Wp)
+
+    def hidden_tile(b, start, j):
+        at = pl.ds(pl.multiple_of(start + j * W, W), W)
         return contract(act_half[b], scaled[at, :], 1, 1)
 
-    for u in range(nt):
+    steps = [(u, h) for u in range(nt) for h in range(H)]
+    for v, (u, h) in enumerate(steps):
         for k, peer in enumerate(cols):
-            @pl.loop(0, Pp // W)
-            def _(j, u=u, k=k, peer=peer):
+            @pl.loop(0, Wp // W)
+            def _(j, u=u, v=v, h=h, k=k, peer=peer):
                 at = pl.ds(pl.multiple_of(j * W, W), W)
-                hp[u, k, :, at] = hidden_tile(tok_block(u), peer, j).astype(half)
-
-            send(hp.at[u, k], xr.at[u, c], x_send.at[u, k], x_recv.at[u, c], {"col": peer})
-    for u in range(nt):
-        b = tok_block(u)
+                hp[v, k, :, at] = hidden_tile(tok_block(u), peer * Pp + h * Wp, j).astype(half)
+
+            send(hp.at[v, k], xr.at[v, c], x_send.at[v, k], x_recv.at[v, c], {"col": peer})
+    for v, (u, h) in enumerate(steps):
         for peer in cols:
-            arrived(xr.at[u, peer], x_recv.at[u, peer], {"col": peer})
+            arrived(xr.at[v, peer], x_recv.at[v, peer], {"col": peer})
         if u > 0:
-            arrived(zr.at[u - 1], z_recv.at[u - 1], right)
-
-        @pl.loop(0, Pp // W)
-        def _(j, u=u, b=b):
+            arrived(zr.at[v - H], z_recv.at[v - H], right)
+
+        @pl.loop(0, Wp // W)
+        def _(j, u=u, v=v, h=h):
             at = pl.ds(pl.multiple_of(j * W, W), W)
-            total = hidden_tile(b, c, j)
+            total = hidden_tile(tok_block(u), c * Pp + h * Wp, j)
             for peer in cols:
-                total = total + xr[u, peer, :, at].astype(wide)
+                total = total + xr[v, peer, :, at].astype(wide)
             if u > 0:
-                total = total + zr[u - 1, :, at].astype(wide)
+                total = total + zr[v - H, :, at].astype(wide)
             if u < nt - 1:
-                zs[u, :, at] = total.astype(half)
+                zs[v, :, at] = total.astype(half)
             else:
-                hid[c, :, at] = total.astype(half)
+                hid[c * H + h, :, at] = total.astype(half)
 
         if u < nt - 1:
-            send(zs.at[u], zr.at[u], z_send.at[u], z_recv.at[u], right)
-    for k, peer in enumerate(cols):
-        send(hid.at[c], hid.at[c], h_send.at[k], h_recv.at[c], {"col": peer})
+            send(zs.at[v], zr.at[v], z_send.at[v], z_recv.at[v], right)
+        else:
+            for k, peer in enumerate(cols):
+                piece = hid.at[c * H + h]
+                send(piece, piece, h_send.at[h, k], h_recv.at[c * H + h], {"col": peer})
     gb_in.wait()
-    for peer in cols:
-        arrived(hid.at[peer], h_recv.at[peer], {"col": peer})
+    for h in range(H):
+        for peer in cols:
+            arrived(hid.at[peer * H + h], h_recv.at[peer * H + h], {"col": peer})
     V = min(256, Oc)
     twin = r + 1 - 2 * lax.rem(r, 2)
     far = [lax.rem(r + 2 * k, nr) for k in range(1, nr // 2)]
@@ -288,9 +306,9 @@
         @pl.loop(0, Oc // V)
         def _(i, j=j):
             at = pl.ds(pl.multiple_of(j * Oc + i * V, V), V)
-            total = contract(hid[0], gb[at, pl.ds(0, Pp)], 1, 1)
-            for k in range(1, nc):
-                total = total + contract(hid[k], gb[at, pl.ds(k * Pp, Pp)], 1, 1)
+            total = contract(hid[0], gb[at, pl.ds(0, Wp)], 1, 1)
+            for k in range(1, nc * H):
+                total = total + contract(hid[k], gb[at, pl.ds(k * Wp, Wp)], 1, 1)
             osend[j, :, pl.ds(pl.multiple_of(i * V, V), V)] = total.astype(half)
 
         for k, peer in enumerate(rows):
@@ -312,17 +330,23 @@
         copy.wait_send()
 
 
+def halves(extent):
+    return 2 if extent >= 512 else 1
+
+
 def project(nt, nr, nc, activations, gradients, act_basis, grad_basis):
     R, F = activations.shape
     Q = act_basis.shape[1]
     G, Pn = grad_basis.shape
     Fp, Pp, S = F // nc, Pn // nc, R // nr
+    H = halves(Pp)
+    Wp = Pp // H
     dma = pltpu.SemaphoreType.DMA
     return pl.pallas_call(
         functools.partial(project_kernel, nt, nr, nc),
         out_shape=(
             jax.ShapeDtypeStruct((nt, R, Q), half),
-            jax.ShapeDtypeStruct((nc, nt, R, Pp), half),
+            jax.ShapeDtypeStruct((nc * H, nt, R, Wp), half),
         ),
         in_specs=[pl.BlockSpec(memory_space=pl.ANY)] * 4,
         out_specs=[pl.BlockSpec(memory_space=pltpu.VMEM)] * 2,
@@ -331,15 +355,15 @@
             pltpu.VMEM((R, G), half),
             pltpu.VMEM((nc, Fp, Q), half),
             pltpu.VMEM((nc, G, Pp), half),
-            pltpu.VMEM((nc, R, Pp), half),
-            pltpu.VMEM((R, Pp), wide),
-            pltpu.VMEM((nc, R, Pp), half),
+            pltpu.VMEM((nc * H, R, Wp), half),
+            pltpu.VMEM((H, R, Wp), wide),
+            pltpu.VMEM((nc * H, R, Wp), half),
             pltpu.VMEM((nt, R, Q), half),
             pltpu.VMEM((nt, nr, S, Q), half),
             dma((3 * nc + 1,)),
-            dma((nc,)), dma((nc,)),
+            dma((nc * H,)), dma((nc * H,)),
             dma((nt,)), dma((nt,)), dma((nc,)), dma((nc,)), dma((nt, nc)), dma((nt, nc)),
-            dma((nt,)), dma((nt,)), dma((nt, nc)), dma((nt, nc)),
+            dma((nt * H,)), dma((nt * H,)), dma((nt * H, nc)), dma((nt * H, nc)),
             dma((nt, nr)), dma((nt, nr)), dma((nt, nr)), dma((nt, nr)),
         ],
         compiler_params=pltpu.CompilerParams(
@@ -390,7 +414,9 @@
     R = act_half.shape[1]
     G, Pn = grad_basis.shape
     Pp, S = Pn // nc, R // nr
-    chunks = 4
+    H = halves(Pp)
+    Wp = Pp // H
+    chunks = 8
     Oc = G // chunks
     dma = pltpu.SemaphoreType.DMA
     return pl.pallas_call(
@@ -399,16 +425,16 @@
         in_specs=[pl.BlockSpec(memory_space=pltpu.VMEM)] * 2 + [pl.BlockSpec(memory_space=pl.ANY)],
         out_specs=pl.BlockSpec(memory_space=pltpu.VMEM),
         scratch_shapes=[
-            pltpu.VMEM((nt, nc - 1, R, Pp), half),
-            pltpu.VMEM((nt, nc, R, Pp), half),
-            pltpu.VMEM((nt, R, Pp), half),
-            pltpu.VMEM((nt, R, Pp), half),
-            pltpu.VMEM((nc, R, Pp), half),
+            pltpu.VMEM((nt * H, nc - 1, R, Wp), half),
+            pltpu.VMEM((nt * H, nc, R, Wp), half),
+            pltpu.VMEM((nt * H, R, Wp), half),
+            pltpu.VMEM((nt * H, R, Wp), half),
+            pltpu.VMEM((nc * H, R, Wp), half),
             pltpu.VMEM((G, Pn), half),
             pltpu.VMEM((chunks, R, Oc), half),
             pltpu.VMEM((chunks, nr, S, Oc), half),
             dma,
-            dma((nt, nc)), dma((nt, nc)), dma((nt,)), dma((nt,)), dma((nc,)), dma((nc,)),
+            dma((nt * H, nc)), dma((nt * H, nc)), dma((nt * H,)), dma((nt * H,)), dma((H, nc)), dma((nc * H,)),
             dma((chunks, nr)), dma((chunks, nr)), dma((chunks, nr)), dma((chunks, nr)), dma((chunks, nr)),
         ],
         compiler_params=pltpu.CompilerParams(
@@ -421,7 +447,7 @@
 def shards(nt, nr, nc, activations, gradients, act_basis, grad_basis, eigen_noise):
     token_count = activations.shape[0] * nt
     act_half, grad_all = project(nt, nr, nc, activations, gradients, act_basis, grad_basis)
-    grad_all = grad_all.reshape(nc, token_count, -1)
+    grad_all = grad_all.reshape(grad_all.shape[0], token_count, -1)
     scales, scaled = scale(act_half.reshape(token_count, -1), grad_all, eigen_noise)
     return (scales, shift(nt, nr, nc, act_half, scaled, grad_basis))
 

time: 235 us -> 226 us (0.962); the launches traced: 231 us -> 225 us
  Pallas kernels: 227 us -> 222 us
    pallas_call x1, Pallas kernels: 109 us -> 103 us  [shift(): pl.pallas_call(functools.partial(output_kernel, nt, nr, nc), out_shape=ja...]
where the time goes in v3:
time: 226 us; the launch traced here: 225 us
  Pallas kernels  222 us (98%)
  local copies, waits for them, and re-layouts  3.13 us (1%)
    pallas_call x1, Pallas kernels, project(): pl.pallas_call(functools.partial(project_kernel, nt, nr, nc), out_shape=(...  104 us
    pallas_call x1, Pallas kernels, shift(): pl.pallas_call(functools.partial(output_kernel, nt, nr, nc), out_shape=ja...  103 us
    pallas_call x1, Pallas kernels, scale(): pl.pallas_call(functools.partial(scale_kernel, tokens), grid=(nc, steps),...  15 us

profile of v3, /device:TPU:0, one launch (start us, length us, event | category | flops | bytes accessed | tf_op | source)
XLA Modules:
  0.0 225.5 jit_solution(5570420502384734345)
XLA Ops:
  0.6 103.6 %shard_map.68 = (bf16[4,256,1024]{2,1,0:T(8,128)(2,1)}, bf16[4,4,256,512]{3,2,1,0:T(8,128)(2,1)}) custom-call(bf16[256,2048]{1,0:T(8,128)(2,1)} %act_hbm.1, bf16[256,4096]{1,0:T(8,128)(2,1)} %grad_hbm.1, bf16[2048,1024]{1,0:T(8,128)(2,1)} %ab_hbm.1, bf16[4096,2048]{1,0:T(8,128)(2,1)} %gb_hbm.3), custom_call_target="tpu_custom_call" | custom-call | flops 8589934592 | bytes 20971520 | tf_op jit(solution)/shard_map/pallas_call | solution.py:345
  104.2 15.0 %shard_map.69 = (f32[2048,1024]{1,0:T(8,128)}, bf16[2048,1024]{1,0:T(8,128)(2,1)}) custom-call(bf16[4,1024,512]{2,1,0:T(8,128)(2,1)} %bitcast.3, bf16[1024,1024]{1,0:T(8,128)(2,1)} %bitcast.2, f32[2048,1024]{1,0:T(8,128)} %noise.1), custom_call_target="tpu_custom_call" | custom-call | flops 4294967296 | bytes 20971520 | tf_op jit(solution)/shard_map/pallas_call | solution.py:395
  119.2 103.2 %shard_map.70 = bf16[256,4096]{1,0:T(8,128)(2,1)} custom-call(bf16[4,256,1024]{2,1,0:T(8,128)(2,1)} %get-tuple-element.7.act_half, bf16[2048,1024]{1,0:T(8,128)(2,1)} %get-tuple-element.9.scaled, bf16[4096,2048]{1,0:T(8,128)(2,1)} %gb_hbm.3), custom_call_target="tpu_custom_call" | custom-call | flops 4294967296 | bytes 16777216 | tf_op jit(solution)/shard_map/pallas_call | solution.py:422
  222.4 3.1 %copy.8 = bf16[256,4096]{1,0:T(8,128)(2,1)} copy(bf16[256,4096]{1,0:T(8,128)(2,1)} %shard_map.70) | data formatting | bytes 4194304
